TPU v7x, 32 devices: a whole 2x2x4 slice. The times are simulated.
32 devices in a mesh: row: 8 (over z, y), col: 4 (over x, core).
Axes of the slice: x: 2, y: 2, z: 4, core: 2. Of those that a mesh axis runs over, the one named last changes fastest.
Arguments:
- upper_tiles: bfloat16 [256, 17, 4096], P(('row', 'col')), may hold values from -0.51 to 0.51, as said below
- block_columns: int32 [256, 17], P(('row', 'col')), may hold values from -1 to 255, as said below
Outputs:
- new_tiles: float32 [256, 17, 4096], P(('row', 'col'))
- occupancy: float32 [], replicated
Inputs may be any that keep to these rules, and one draw needn't show every extreme that they name: `block_columns`: slot 0 of block row i holds i. The following slots hold distinct block columns (i + s) mod 256 with 1 <= s <= 16, in increasing s, and the remaining slots hold -1. Some block rows fill all 17 slots. `upper_tiles`: the block in slot 0 is symmetric.
All inputs are finite; a program needn't handle non-finite values.
Results may differ from a plain program's by a relative error of at most 0.0003.
Values may be sent and summed in bfloat16 or wider, within the bound.
A program may use at most 128 MiB of HBM per device.

v0:
```python
import math

import jax
import jax.numpy as jnp
import numpy as np
from jax import lax
from jax.sharding import PartitionSpec as P


def from_behind(shard, axis, by):
    length = lax.axis_size(axis)
    return lax.ppermute(shard, axis, [(i, (i + by) % length) for i in range(length)])


def entry_tables(rows_dev, half):
    band_width = half + 1
    window = rows_dev + 2 * half
    zero_index = window * band_width
    flipped_base = zero_index + 1

    def lookup(row_pos, col_pos):
        if col_pos >= row_pos and col_pos - row_pos <= half:
            return row_pos * band_width + col_pos - row_pos
        if col_pos < row_pos and row_pos - col_pos <= half:
            return flipped_base + col_pos * band_width + row_pos - col_pos
        return zero_index

    left_index = np.zeros((rows_dev, window), np.int32)
    for own_row in range(rows_dev):
        for other_row in range(window):
            left_index[own_row, other_row] = lookup(half + own_row, other_row)
    right_index = np.zeros((window, rows_dev + half), np.int32)
    for other_row in range(window):
        for column_pos in range(rows_dev + half):
            right_index[other_row, column_pos] = lookup(other_row, half + column_pos)
    return (left_index, right_index)


def flip_tiles(tiles, block):
    shaped = tiles.reshape(tiles.shape[:-1] + (block, block))
    return jnp.swapaxes(shaped, -1, -2).reshape(tiles.shape)


def body(upper_tiles, block_columns):
    rows_dev, slots, tile_size = upper_tiles.shape
    half = slots - 1
    block = math.isqrt(tile_size)
    devices = lax.axis_size(("row", "col"))
    nblocks = rows_dev * devices
    span_cols = rows_dev + half
    window_rows = rows_dev + 2 * half
    first_row = lax.axis_index(("row", "col")) * rows_dev
    local_rows = jnp.arange(rows_dev, dtype=jnp.int32)
    row_ids = first_row + local_rows
    slot_range = jnp.arange(slots, dtype=jnp.int32)
    listed = block_columns >= 0
    offsets_of = jnp.mod(block_columns - row_ids[:, None], nblocks)
    pick_band = (listed[:, :, None] & (offsets_of[:, :, None] == slot_range[None, None, :])).astype(
        jnp.bfloat16
    )
    own_band = jnp.einsum(
        "rso,rst->rot", pick_band, upper_tiles, preferred_element_type=jnp.float32
    ).astype(jnp.bfloat16)
    diag_own = upper_tiles[:, 0].astype(jnp.float32).reshape(rows_dev, block, block)
    own_trace = 2.0 * jnp.sum(jnp.diagonal(diag_own, axis1=1, axis2=2))
    reach = -(-half // rows_dev)
    below = []
    above = []
    moving = own_band
    for distance in range(reach):
        moving = from_behind(moving, ("row", "col"), 1)
        below.insert(0, moving)
    moving = own_band
    for distance in range(reach):
        moving = from_behind(moving, ("row", "col"), -1)
        above.append(moving)
    stacked = jnp.concatenate(below + [own_band] + above, axis=0)
    left_np, right_np = entry_tables(rows_dev, half)
    plain = stacked.reshape(window_rows * slots, tile_size)
    blank = jnp.zeros((1, tile_size), jnp.bfloat16)
    flat = jnp.concatenate([plain, blank, flip_tiles(plain, block)], axis=0)
    left = flat[jnp.asarray(left_np)].reshape(rows_dev, window_rows, block, block)
    right = flat[jnp.asarray(right_np)].reshape(window_rows, span_cols, block, block)
    product = jnp.einsum("rjab,jkbc->rkac", left, right, preferred_element_type=jnp.float32)
    product = product.reshape(rows_dev, span_cols, tile_size)
    target = jnp.where(listed, offsets_of + local_rows[:, None], -1)
    pick_new = (target[:, :, None] == jnp.arange(span_cols, dtype=jnp.int32)[None, None, :]).astype(
        jnp.float32
    )
    picked = jnp.einsum(
        "rsk,rkt->rst",
        pick_new,
        product,
        precision=lax.Precision.HIGHEST,
        preferred_element_type=jnp.float32,
    )
    new_tiles = jnp.where(listed[:, :, None], 2.0 * upper_tiles.astype(jnp.float32) - picked, 0.0)
    diag_product = product[local_rows, local_rows].reshape(rows_dev, block, block)
    total = lax.psum(
        own_trace - jnp.sum(jnp.diagonal(diag_product, axis1=1, axis2=2)), ("row", "col")
    )
    occupancy = (total / (nblocks * block)).astype(jnp.float32)
    return (new_tiles, occupancy)


def solution(mesh):
    placed = (P(("row", "col"), None, None), P(("row", "col"), None))
    return jax.shard_map(
        body,
        mesh=mesh,
        in_specs=placed,
        out_specs=(P(("row", "col"), None, None), P()),
        check_vma=False,
    )
```

profile of v0, /device:TPU:1, one launch (start us, length us, event | category | flops | bytes accessed | tf_op | source)
XLA Modules:
  0.0 326.3 jit_solution(8434961072825419353)
XLA Ops:
  1.4 2.8 convolution_convert_fusion
  6.0 2.6 collective-permute-start
  8.6 24.7 %collective-permute-done = bf16[8,17,4096]{2,0,1:T(8,128)(2,1)} collective-permute-done((bf16[8,17,4096]{2,0,1:T(8,128)(2,1)}, bf16[8,17,4096]{2,0,1:T(8,128)(2,1)}, u32[]{:S(2)}, u32[]{:S(2)}) %collective-permute-start) | collective-permute-done | bytes 1114144 | tf_op jit(solution)/shard_map/ppermute | solution.py:12
  33.3 2.5 collective-permute-start.1
  36.6 1.9 copy.34
  41.5 18.9 %collective-permute-done.1 = bf16[8,17,4096]{2,0,1:T(8,128)(2,1)} collective-permute-done((bf16[8,17,4096]{2,0,1:T(8,128)(2,1)}, bf16[8,17,4096]{2,0,1:T(8,128)(2,1)}, u32[]{:S(2)}, u32[]{:S(2)}) %collective-permute-start.1) | collective-permute-done | bytes 1114144 | tf_op jit(solution)/shard_map/ppermute | solution.py:12
  60.5 3.1 copy_dynamic-update-slice_fusion.3
  63.6 3.1 copy_dynamic-update-slice_fusion.2
  69.7 1.8 copy_dynamic-update-slice_fusion
  71.6 8.1 %reshape.33 = bf16[680,4096]{1,0:T(8,128)(2,1)} reshape(bf16[40,17,4096]{2,1,0:T(8,128)(2,1)} %copy_dynamic-update-slice_fusion) | data formatting | bytes 11141120 | tf_op jit(solution)/shard_map/reshape | solution.py:79
  79.7 16.5 %reshape_reshape.3 = bf16[680,64,64]{2,1,0:T(8,128)(2,1)} reshape(bf16[40,17,4096]{2,1,0:T(8,128)(2,1)} %copy_dynamic-update-slice_fusion) | data formatting | bytes 11141120 | tf_op jit(solution)/shard_map/reshape;reshape | solution.py:40
  96.2 19.3 %copy.30 = bf16[680,64,64]{0,2,1:T(8,128)(2,1)} copy(bf16[680,64,64]{1,2,0:T(8,128)(2,1)} %bitcast.21) | data formatting | bytes 11141120 | tf_op jit(solution)/shard_map/transpose | solution.py:41
  115.5 8.3 %copy.31 = bf16[680,4096]{1,0:T(8,128)(2,1)} copy(bf16[680,4096]{0,1:T(8,128)(2,1)} %bitcast.22) | data formatting | bytes 11141120 | tf_op jit(solution)/shard_map/reshape | solution.py:41
  123.7 51.6 %concatenate.15 = bf16[1361,4096]{1,0:T(8,128)(2,1)} concatenate(bf16[680,4096]{1,0:T(8,128)(2,1)} %reshape.33, bf16[1,4096]{1,0:T(2,128)(2,1)S(1)} %broadcast_in_dim.43, bf16[680,4096]{1,0:T(8,128)(2,1)} %copy.31), dimensions={0} | concatenate | bytes 22298624 | tf_op jit(solution)/shard_map/concatenate | solution.py:81
  175.4 13.1 %gather_fusion.1 = bf16[320,4096]{1,0:T(8,128)(2,1)S(1)} fusion(bf16[1361,4096]{1,0:T(8,128)(2,1)} %concatenate.15, s32[1024]{0:T(1024)S(1)} %get-tuple-element.11), kind=kCustom, calls=%fused_computation.1 | custom fusion | bytes 5244160 | tf_op jit(solution)/shard_map/gather | solution.py:82
  188.5 6.7 %reshape.79 = bf16[8,40,64,64,1]{3,2,1,0,4:T(8,128)(2,1)} reshape(bf16[320,4096]{1,0:T(8,128)(2,1)S(1)} %gather_fusion.1) | data formatting | bytes 5242880 | tf_op jit(solution)/shard_map/reshape | solution.py:82
  195.1 20.8 %gather_fusion = bf16[960,4096]{1,0:T(8,128)(2,1)} fusion(bf16[1361,4096]{1,0:T(8,128)(2,1)} %concatenate.15, s32[1024]{0:T(1024)S(1)} %get-tuple-element.12), kind=kCustom, calls=%fused_computation | custom fusion | bytes 15732480 | tf_op jit(solution)/shard_map/gather | solution.py:83
  215.9 22.0 %reshape.35 = bf16[40,24,64,64]{3,2,1,0:T(8,128)(2,1)} reshape(bf16[960,4096]{1,0:T(8,128)(2,1)} %gather_fusion) | data formatting | bytes 15728640 | tf_op jit(solution)/shard_map/reshape | solution.py:83
  237.9 22.3 %fusion.3 = f32[8,24,64,64]{2,3,0,1:T(8,128)} fusion(bf16[8,40,64,64,1]{3,2,1,0,4:T(8,128)(2,1)} %reshape.79, bf16[40,24,64,64]{3,2,1,0:T(8,128)(2,1)} %reshape.35), kind=kOutput, calls=%fused_computation.10 | convolution fusion | flops 4026531840 | bytes 13631488 | tf_op jit(solution)/shard_map/rjab,jkbc->rkac/dot_general | solution.py:84
  260.2 6.6 %copy.33 = f32[8,24,64,64]{3,2,1,0:T(8,128)} copy(f32[8,24,64,64]{2,3,0,1:T(8,128)} %fusion.3) | data formatting | bytes 6291456 | tf_op jit(solution)/shard_map/rjab,jkbc->rkac/transpose | solution.py:84
  266.8 4.7 %reshape.37 = f32[8,24,4096]{2,1,0:T(8,128)S(1)} reshape(f32[8,24,64,64]{3,2,1,0:T(8,128)} %copy.33) | data formatting | bytes 6291456 | tf_op jit(solution)/shard_map/reshape | solution.py:85
  271.5 5.8 %fusion.2 = f32[8,17,4096]{2,1,0:T(8,128)} fusion(f32[8,24,4096]{2,1,0:T(8,128)S(1)} %reshape.37, bf16[8,17,4096]{2,0,1:T(8,128)(2,1)} %param.4, pred[8,17]{1,0:T(8,128)(4,1)S(1)} %get-tuple-element.9, s32[8,17]{1,0:T(8,128)S(1)} %get-tuple-element.8), kind=kOutput, calls=%fused_computation.8 | convolution fusion | flops 162663616 | bytes 6488744 | tf_op jit(solution)/shard_map/rsk,rkt->rst/dot_general | solution.py:90
  280.8 4.5 %copy.36 = f32[8,17,4096]{2,0,1:T(8,128)} copy(f32[8,17,4096]{2,1,0:T(8,128)} %fusion.2) | data formatting | bytes 4456448
  285.3 39.2 %psum.7 = f32[]{:T(128)} all-reduce(f32[]{:T(128)S(6)} %sub.17), channel_id=1, replica_groups=mesh['row'=8,'col'=4] {'row','col'}, use_global_device_ids=true, to_apply=%region_2.3 | all-reduce | flops 1 | bytes 8 | tf_op jit(solution)/shard_map/psum | solution.py:99
  (24 shorter events, 11.4 us)
Async XLA Ops:
  4.2 37.2 %copy-start = (s32[960]{0:T(1024)S(1)}, s32[960]{0:T(1024)}, u32[]{:S(2)}) copy-start(s32[960]{0:T(1024)} %constant.112) | copy-start | bytes 11524
  4.3 37.2 %copy-start.1 = (s32[320]{0:T(512)S(1)}, s32[320]{0:T(512)}, u32[]{:S(2)}) copy-start(s32[320]{0:T(512)} %constant.113) | copy-start | bytes 3844
  6.0 27.3 %collective-permute-start = (bf16[8,17,4096]{2,0,1:T(8,128)(2,1)}, bf16[8,17,4096]{2,0,1:T(8,128)(2,1)}, u32[]{:S(2)}, u32[]{:S(2)}) collective-permute-start(bf16[8,17,4096]{2,0,1:T(8,128)(2,1)} %copy.24), channel_id=1, source_target_pairs={{0,1},{1,2},{2,3},{3,4},{4,5},{5,6},{6,7},{7,8},{8,9},{9,10},{10,1... | collective-permute-start | bytes 3342344 | tf_op jit(solution)/shard_map/ppermute | solution.py:12
  8.6 32.9 %collective-permute-start.2 = (bf16[8,17,4096]{2,0,1:T(8,128)(2,1)}, bf16[8,17,4096]{2,0,1:T(8,128)(2,1)S(1)}, u32[]{:S(2)}, u32[]{:S(2)}) collective-permute-start(bf16[8,17,4096]{2,0,1:T(8,128)(2,1)} %copy.24), channel_id=1, source_target_pairs={{0,31},{1,0},{2,1},{3,2},{4,3},{5,4},{6,5},{7,6},{8,7},{9,8},{10,9... | collective-permute-start | bytes 3342344 | tf_op jit(solution)/shard_map/ppermute | solution.py:12
  33.3 27.2 %collective-permute-start.1 = (bf16[8,17,4096]{2,0,1:T(8,128)(2,1)}, bf16[8,17,4096]{2,0,1:T(8,128)(2,1)}, u32[]{:S(2)}, u32[]{:S(2)}) collective-permute-start(bf16[8,17,4096]{2,0,1:T(8,128)(2,1)} %collective-permute-done), channel_id=1, source_target_pairs={{0,1},{1,2},{2,3},{3,4},{4,5},{5,6},{6,7},{7,8},{8,9},{9,10},{10,1... | collective-permute-start | bytes 3342344 | tf_op jit(solution)/shard_map/ppermute | solution.py:12
  41.4 28.3 %collective-permute-start.3 = (bf16[8,17,4096]{2,0,1:T(8,128)(2,1)S(1)}, bf16[8,17,4096]{2,0,1:T(8,128)(2,1)S(1)}, u32[]{:S(2)}, u32[]{:S(2)}) collective-permute-start(bf16[8,17,4096]{2,0,1:T(8,128)(2,1)S(1)} %collective-permute-done.2), channel_id=1, source_target_pairs={{0,31},{1,0},{2,1},{3,2},{4,3},{5,4},{6,5},{7,6},{8,7},{9,8},{10,9... | collective-permute-start | bytes 3342344 | tf_op jit(solution)/shard_map/ppermute | solution.py:12
where the time goes:
time: 331 us; the launch traced here: 326 us
  local copies, waits for them, and re-layouts  201 us (61%)
  waiting for transfers between devices  43.6 us (13%)
  blocking collectives  39.2 us (12%)
  matrix products  31 us (9%)
  starting transfers between devices  5.14 us (2%)
  between operations  3.84 us (1%)
    concatenate x1, local copies, waits for them, and re-layouts, body(): flat = jnp.concatenate([plain, blank, flip_tiles(plain, block)], axis=0)  51.6 us
    ppermute x4, waiting for transfers between devices, from_behind(): lax.ppermute(shard, axis, [(i, (i + by) % length) for i in range(length)])  43.6 us
    psum x1, blocking collectives, body(): lax.psum(own_trace - jnp.sum(jnp.diagonal(diag_product, axis1=1, axis2=2)...  39.2 us
    dot_general x1, matrix products, body(): jnp.einsum('rjab,jkbc->rkac', left, right, preferred_element_type=jnp.flo...  22.3 us
    reshape x1, local copies, waits for them, and re-layouts, body(): flat[jnp.asarray(right_np)].reshape(window_rows, span_cols, block, block)  22 us
    gather x1, local copies, waits for them, and re-layouts, body(): flat[jnp.asarray(right_np)].reshape(window_rows, span_cols, block, block)  20.8 us
    transpose x1, local copies, waits for them, and re-layouts, flip_tiles(): return jnp.swapaxes(shaped, -1, -2).reshape(tiles.shape)  19.3 us
    another operation x1, local copies, waits for them, and re-layouts, flip_tiles(): shaped = tiles.reshape(tiles.shape[:-1] + (block, block))  16.5 us
  transfers between devices with their start and end apart: 4, of which 2 were waited for; matrix products, arithmetic and copies ran while one was open for 4% of the time, Pallas kernels for 0%

commit v1 on v0

v1 whole, which is shorter than its diff:
```python
import functools
import math

import jax
import jax.numpy as jnp
from jax import lax
from jax.experimental import pallas as pl
from jax.experimental.pallas import tpu as pltpu
from jax.sharding import PartitionSpec as P

MESH = pl.DeviceIdType.MESH
F32 = jnp.float32
BF16 = jnp.bfloat16


def dot(a, b, ca, cb):
    return lax.dot_general(a, b, (((ca,), (cb,)), ((), ())), preferred_element_type=F32)


def kernel(
    dims,
    x_ref,
    cols_ref,
    out_ref,
    tab,
    stage,
    flat,
    own,
    sym,
    e1,
    f1,
    e2,
    d1,
    c1,
    d2,
    prod,
    send_sem,
    recv_sem,
):
    rows, slots, block, nrow, ncol = dims
    half = slots - 1
    width = rows * block
    span = rows + half
    devices = nrow * ncol
    nblocks = devices * rows
    lanes = 2 * block
    me = lax.axis_index("row") * ncol + lax.axis_index("col")

    def at(shift):
        other = lax.rem(me + shift + devices, devices)
        return (lax.div(other, ncol), lax.rem(other, ncol))

    barrier = pltpu.get_barrier_semaphore()
    for shift in (-2, -1, 1, 2):
        pl.semaphore_signal(barrier, inc=1, device_id=at(shift), device_id_type=MESH)

    def fill(r, carry):
        row_id = me * rows + r
        for t in range(rows + span):
            tab[r, t] = jnp.int32(-1)
        tab[r, rows] = jnp.where(cols_ref[r, 0] >= 0, 0, -1).astype(jnp.int32)
        slot = jnp.int32(1)
        for offset in range(1, half + 1):
            want = row_id + offset
            want = jnp.where(want >= nblocks, want - nblocks, want)
            hit = cols_ref[r, jnp.minimum(slot, half)] == want
            tab[r, rows + offset] = jnp.where(hit, slot, -1)
            slot = slot + hit.astype(jnp.int32)
        return carry

    lax.fori_loop(0, rows, fill, 0)

    left = lax.broadcasted_iota(jnp.int32, (block // 2, lanes), 1) < block

    def unpack(r, carry):
        for m in range(span // 2):
            pair = []
            for k in (2 * m, 2 * m + 1):
                slot = tab[r, rows + k - r]
                tile = x_ref[jnp.clip(slot, 0, half), r].astype(F32)
                pair.append(jnp.where(slot >= 0, tile, 0.0))
            even = jnp.where(left, pair[0], pltpu.roll(pair[1], block, 1))
            odd = jnp.where(left, pltpu.roll(pair[0], block, 1), pair[1])
            stage[m, pl.ds(0, block // 2, stride=2), :] = even
            stage[m, pl.ds(1, block // 2, stride=2), :] = odd
        for m in range(span // 2):
            own[pl.ds(pl.multiple_of(r * block, block), block), m * lanes : (m + 1) * lanes] = stage[m].astype(BF16)
        return carry

    lax.fori_loop(0, rows, unpack, 0)

    for q in range(rows // 2):
        strip = pl.ds(q * lanes, lanes)
        if q:
            d1[strip, : q * lanes] = jnp.zeros((lanes, q * lanes), BF16)
            d2[strip, : q * lanes] = jnp.zeros((lanes, q * lanes), BF16)
        if (q + 1) * lanes < width:
            f1[strip, (q + 1) * lanes :] = jnp.zeros((lanes, width - (q + 1) * lanes), BF16)
            e2[strip, (q + 1) * lanes :] = jnp.zeros((lanes, width - (q + 1) * lanes), BF16)

    pl.semaphore_wait(barrier, 4)

    copies = {}
    plan = (
        ("e1", e1, 1, 1, "full"),
        ("c1", c1, 1, -1, "full"),
        ("f1", f1, 2, 1, "low"),
        ("d1", d1, 0, -1, "up"),
        ("e2", e2, 2, 2, "low"),
        ("d2", d2, 0, -2, "up"),
    )
    for index, (name, target, part, shift, kind) in enumerate(plan):
        copies[name] = []
        for q in range(rows // 2):
            lo = q * lanes if kind == "up" else 0
            size = {"full": width, "up": width - q * lanes, "low": (q + 1) * lanes}[kind]
            copy = pltpu.make_async_remote_copy(
                src_ref=own.at[pl.ds(q * lanes, lanes), pl.ds(part * width + lo, size)],
                dst_ref=target.at[pl.ds(q * lanes, lanes), pl.ds(lo, size)],
                send_sem=send_sem.at[index, q],
                recv_sem=recv_sem.at[index, q],
                device_id=at(shift),
                device_id_type=MESH,
            )
            copy.start()
            copies[name].append(copy)

    def arrived(*names):
        for name in names:
            for copy in copies[name]:
                copy.wait_recv()

    row_block = lax.broadcasted_iota(jnp.int32, (width, width), 0) // block
    col_block = lax.broadcasted_iota(jnp.int32, (width, width), 1) // block
    upper = row_block <= col_block

    def symmetric(d):
        d = d.astype(F32)
        return jnp.where(upper, d, d.T).astype(BF16)

    sym[...] = symmetric(own[:, :width])
    a = own.at[:, width : 2 * width]
    b = own.at[:, 2 * width :]
    p0, p1, p2 = (prod.at[:, i * width : (i + 1) * width] for i in range(3))
    p0[...] = dot(sym[...], sym[...], 1, 0) + dot(a[...], a[...], 1, 1) + dot(b[...], b[...], 1, 1)
    p1[...] = dot(sym[...], a[...], 1, 0)
    p2[...] = dot(sym[...], b[...], 1, 0)

    arrived("e1")
    p0[...] += dot(e1[...], e1[...], 0, 0)
    arrived("c1")
    p1[...] += dot(b[...], c1[...], 1, 1)
    p2[...] += dot(a[...], c1[...], 1, 0)
    arrived("f1")
    p1[...] += dot(e1[...], f1[...], 0, 0)
    arrived("d1")
    sym[...] = symmetric(d1[...])
    p1[...] += dot(a[...], sym[...], 1, 0)
    arrived("e2")
    p0[...] += dot(e2[...], e2[...], 0, 0)
    arrived("d2")
    sym[...] = symmetric(d2[...])
    p2[...] += dot(b[...], sym[...], 1, 0)

    def pack(r, carry):
        rs = pl.ds(pl.multiple_of(r * block, block), block)
        for m in range(span // 2):
            cs = slice(m * lanes, (m + 1) * lanes)
            stage[m] = 2.0 * own[rs, cs].astype(F32) - prod[rs, cs]
        for m in range(span // 2):
            even = stage[m, pl.ds(0, block // 2, stride=2), :]
            odd = stage[m, pl.ds(1, block // 2, stride=2), :]
            flat[2 * m] = jnp.where(left, even, pltpu.roll(odd, block, 1))
            flat[2 * m + 1] = jnp.where(left, pltpu.roll(even, block, 1), odd)
        row_id = me * rows + r
        for s in range(slots):
            column = cols_ref[r, s]
            offset = column - row_id
            offset = jnp.where(offset < 0, offset + nblocks, offset)
            offset = jnp.where(column >= 0, jnp.minimum(offset, half), 0)
            out_ref[s, r] = jnp.where(column >= 0, flat[r + offset], 0.0)
        return carry

    lax.fori_loop(0, rows, pack, 0)

    for group in copies.values():
        for copy in group:
            copy.wait_send()


def body(nrow, ncol, upper_tiles, block_columns):
    rows, slots, tile_size = upper_tiles.shape
    block = math.isqrt(tile_size)
    half = slots - 1
    assert half == 2 * rows and rows % 2 == 0 and 2 * block == 128
    lanes = 2 * block
    width = rows * block
    span = rows + half

    listed = block_columns >= 0
    tiles = upper_tiles.astype(F32)
    weight = jnp.where(listed, jnp.where(jnp.arange(slots) == 0, 1.0, 2.0), 0.0)
    squares = jnp.sum(tiles * tiles * weight[:, :, None])
    on_diagonal = (jnp.arange(tile_size) % (block + 1) == 0) & True
    doubled = 2.0 * jnp.sum(jnp.where(on_diagonal, tiles[:, 0], 0.0))
    total = lax.psum(doubled - squares, ("row", "col"))
    occupancy = (total / (nrow * ncol * rows * block)).astype(F32)

    square = pltpu.VMEM((width, width), BF16)
    new = pl.pallas_call(
        functools.partial(kernel, (rows, slots, block, nrow, ncol)),
        out_shape=jax.ShapeDtypeStruct((slots, rows, block // 2, lanes), F32),
        in_specs=[pl.BlockSpec(memory_space=pltpu.VMEM), pl.BlockSpec(memory_space=pltpu.SMEM)],
        out_specs=pl.BlockSpec(memory_space=pltpu.VMEM),
        scratch_shapes=[
            pltpu.SMEM((rows, rows + span), jnp.int32),
            pltpu.VMEM((span // 2, block, lanes), F32),
            pltpu.VMEM((span, block // 2, lanes), F32),
            pltpu.VMEM((width, 3 * width), BF16),
            square,
            square,
            square,
            square,
            square,
            square,
            square,
            pltpu.VMEM((width, 3 * width), F32),
            pltpu.SemaphoreType.DMA((6, rows // 2)),
            pltpu.SemaphoreType.DMA((6, rows // 2)),
        ],
        compiler_params=pltpu.CompilerParams(
            collective_id=0, has_side_effects=True, vmem_limit_bytes=48 * 1024 * 1024
        ),
        cost_estimate=pl.CostEstimate(
            flops=24 * width**3, bytes_accessed=6 * rows * slots * tile_size, transcendentals=0
        ),
    )(upper_tiles.swapaxes(0, 1).reshape(slots, rows, block // 2, lanes), block_columns)
    return new.reshape(slots, rows, tile_size).swapaxes(0, 1), occupancy


def solution(mesh):
    placed = (P(("row", "col"), None, None), P(("row", "col"), None))
    return jax.shard_map(
        functools.partial(body, mesh.shape["row"], mesh.shape["col"]),
        mesh=mesh,
        in_specs=placed,
        out_specs=(P(("row", "col"), None, None), P()),
        check_vma=False,
    )
```

time: 331 us -> 91.4 us (0.28)
  local copies, waits for them, and re-layouts: 201 us -> 3.35 us
  waiting for transfers between devices: 43.6 us -> 0 us
  Pallas kernels: 0 us -> 41 us
  matrix products: 31 us -> 0 us
  starting transfers between devices: 5.14 us -> 0 us
    concatenate x2 -> x0, local copies, waits for them, and re-layouts: 53.5 us -> none  [the longest x1 51.6 us: body(): flat = jnp.concatenate([plain, blank, flip_tiles(plain, block)], axis=0)]
    reshape x6 -> x1, local copies, waits for them, and re-layouts: 50.3 us -> 1.76 us  [body(): return (new.reshape(slots, rows, tile_size).swapaxes(0, 1), occupancy)]
    ppermute x4 -> x0, waiting for transfers between devices: 43.6 us -> none  [from_behind(): lax.ppermute(shard, axis, [(i, (i + by) % length) for i in range(length)])]
    pallas_call x0 -> x1, Pallas kernels: none -> 41 us  [body(): pl.pallas_call(functools.partial(kernel, (rows, slots, block, nrow, ncol)...]
    gather x5 -> x0, local copies, waits for them, and re-layouts: 37 us -> none  [the longest x1 20.8 us: body(): flat[jnp.asarray(right_np)].reshape(window_rows, span_cols, block, block)]
    dot_general x3 -> x0, matrix products: 31 us -> none  [the longest x1 22.3 us: body(): jnp.einsum('rjab,jkbc->rkac', left, right, preferred_element_type=jnp.flo...]
    transpose x2 -> x0, local copies, waits for them, and re-layouts: 25.9 us -> none  [the longest x1 19.3 us: flip_tiles(): return jnp.swapaxes(shaped, -1, -2).reshape(tiles.shape)]
    another operation x1 -> x0, local copies, waits for them, and re-layouts: 16.5 us -> none  [flip_tiles(): shaped = tiles.reshape(tiles.shape[:-1] + (block, block))]
  transfers between devices with their start and end apart: 4 -> 0, of which waited for: 2 -> 0; matrix products, arithmetic and copies ran while one was open for 4% -> 0% of each run, Pallas kernels for 0% -> 0%
where the time goes in v1:
time: 91.4 us; the launch traced here: 89.8 us
  Pallas kernels  41 us (45%)
  blocking collectives  39.5 us (43%)
  between operations  3.78 us (4%)
  local copies, waits for them, and re-layouts  3.35 us (4%)
  other arithmetic  2.18 us (2%)
    pallas_call x1, Pallas kernels, body(): pl.pallas_call(functools.partial(kernel, (rows, slots, block, nrow, ncol)...  41 us
    psum x1, blocking collectives, body(): total = lax.psum(doubled - squares, ('row', 'col'))  39.5 us

profile of v1, /device:TPU:1, one launch (start us, length us, event | category | flops | bytes accessed | tf_op | source)
XLA Modules:
  0.0 89.8 jit_solution(18360242866666751005)
XLA Ops:
  0.6 0.0 copy-start
  0.6 1.5 %copy.7 = bf16[17,8,32,128]{3,2,1,0:T(8,128)(2,1)S(1)} copy(bf16[17,8,32,128]{3,1,2,0:T(8,128)(2,1)} %bitcast.16) | data formatting | bytes 2228224
  2.1 0.0 copy-done
  2.1 41.0 %shard_map.41 = f32[17,8,32,128]{3,2,1,0:T(8,128)S(1)} custom-call(bf16[17,8,32,128]{3,2,1,0:T(8,128)(2,1)S(1)} %copy.7, s32[8,17]{1,0:T(8,128)S(1)} %copy-done), custom_call_target="tpu_custom_call" | custom-call | flops 3221225472 | bytes 3342336 | tf_op jit(solution)/shard_map/pallas_call | solution.py:210
  43.2 0.0 copy-start.1
  43.2 1.8 %reshape.12 = f32[17,8,4096]{2,1,0:T(8,128)} reshape(f32[17,8,32,128]{3,2,1,0:T(8,128)S(1)} %shard_map.41) | data formatting | bytes 4456448 | tf_op jit(solution)/shard_map/reshape | solution.py:238
  44.9 0.0 copy-done.1
  44.9 0.2 convert_element_type.3
  45.2 0.6 fusion.1
  46.5 0.1 copy.4
  46.6 1.3 %multiply_reduce_fusion = f32[]{:T(128)} fusion(f32[8,17]{0,1:T(8,128)S(1)} %copy.4, bf16[8,17,4096]{2,0,1:T(8,128)(2,1)S(1)} %copy-done.1), kind=kLoop, calls=%fused_computation | loop fusion | flops 2228223 | bytes 1114660 | tf_op jit(solution)/shard_map/reduce_sum | solution.py:203
  48.5 39.5 %psum.7 = f32[]{:T(128)} all-reduce(f32[]{:T(128)S(6)} %sub.3), channel_id=1, replica_groups=mesh['row'=8,'col'=4] {'row','col'}, use_global_device_ids=true, to_apply=%region_2.3 | all-reduce | flops 1 | bytes 8 | tf_op jit(solution)/shard_map/psum | solution.py:206
  (3 shorter events, 0.0 us)
Async XLA Ops:
  0.6 1.5 %copy-start = (s32[8,17]{1,0:T(8,128)S(1)}, s32[8,17]{1,0:T(8,128)}, u32[]{:S(2)}) copy-start(s32[8,17]{1,0:T(8,128)} %cols_ref.1) | copy-start | bytes 1636
  43.2 1.8 %copy-start.1 = (bf16[8,17,4096]{2,0,1:T(8,128)(2,1)S(1)}, bf16[8,17,4096]{2,0,1:T(8,128)(2,1)}, u32[]{:S(2)}) copy-start(bf16[8,17,4096]{2,0,1:T(8,128)(2,1)} %param.2) | copy-start | bytes 3342340

commit v2 on v1

v2 whole, which is shorter than its diff:
```python
import functools
import math

import jax
import jax.numpy as jnp
from jax import lax
from jax.experimental import pallas as pl
from jax.experimental.pallas import tpu as pltpu
from jax.sharding import PartitionSpec as P

MESH = pl.DeviceIdType.MESH
F32 = jnp.float32
BF16 = jnp.bfloat16


def dot(a, b, ca, cb):
    return lax.dot_general(a, b, (((ca,), (cb,)), ((), ())), preferred_element_type=F32)


def kernel(
    dims,
    x_ref,
    cols_ref,
    out_ref,
    occupancy_ref,
    tab,
    stage,
    flat,
    own,
    e1,
    f1,
    e2,
    d1,
    c1,
    d2,
    prod,
    col_parts,
    row_parts,
    send_sem,
    recv_sem,
    col_send,
    col_recv,
    row_send,
    row_recv,
):
    rows, slots, block, nrow, ncol = dims
    half = slots - 1
    width = rows * block
    span = rows + half
    devices = nrow * ncol
    nblocks = devices * rows
    lanes = 2 * block
    strips = rows // 2
    my_row = lax.axis_index("row")
    my_col = lax.axis_index("col")
    me = my_row * ncol + my_col
    even_device = lax.rem(my_col, 2) == 0

    def at(shift):
        other = lax.rem(me + shift + devices, devices)
        return (lax.div(other, ncol), lax.rem(other, ncol))

    def col_peer(d):
        return lax.rem(my_col + d, ncol)

    def row_peer(d):
        return lax.rem(my_row + d, nrow)

    barrier = pltpu.get_barrier_semaphore()
    peers = [at(shift) for shift in (-2, -1, 1, 2)]
    peers += [(my_row, col_peer(d)) for d in range(1, ncol)]
    peers += [(row_peer(d), my_col) for d in range(1, nrow)]
    for peer in peers:
        pl.semaphore_signal(barrier, inc=1, device_id=peer, device_id_type=MESH)

    def fill(r, carry):
        row_id = me * rows + r
        tab[r, 0] = jnp.where(cols_ref[r, 0] >= 0, 0, -1).astype(jnp.int32)
        slot = jnp.int32(1)
        for offset in range(1, half + 1):
            want = row_id + offset
            want = jnp.where(want >= nblocks, want - nblocks, want)
            hit = cols_ref[r, jnp.minimum(slot, half)] == want
            tab[r, offset] = jnp.where(hit, slot, -1)
            slot = slot + hit.astype(jnp.int32)
        return carry

    lax.fori_loop(0, rows, fill, 0)

    sub = lax.broadcasted_iota(jnp.int32, (block // 2, lanes), 0)
    lane = lax.broadcasted_iota(jnp.int32, (block // 2, lanes), 1)
    left = lane < block
    on_diagonal = lane == 2 * sub + jnp.where(left, 0, block + 1)

    targets = {"f1": (f1, 2, 1, "low"), "d1": (d1, 0, -1, "up"), "e2": (e2, 2, 2, "low"),
               "d2": (d2, 0, -2, "up"), "e1": (e1, 1, 1, "full"), "c1": (c1, 1, -1, "full")}
    order = tuple(targets)

    def ranges(kind, q):
        lo = q * lanes if kind == "up" else 0
        return lo, {"full": width, "up": width - q * lanes, "low": (q + 1) * lanes}[kind]

    def strip_copy(name, q):
        target, part, shift, kind = targets[name]
        lo, size = ranges(kind, q)
        return pltpu.make_async_remote_copy(
            src_ref=own.at[pl.ds(q * lanes, lanes), pl.ds(part * width + lo, size)],
            dst_ref=target.at[pl.ds(q * lanes, lanes), pl.ds(lo, size)],
            send_sem=send_sem.at[order.index(name), q],
            recv_sem=recv_sem.at[order.index(name), q],
            device_id=at(shift),
            device_id_type=MESH,
        )

    def forward_copy(name, q):
        source, goal, shift = (f1, "e2", 1) if name == "f1" else (d1, "d2", -1)
        lo, size = ranges(targets[name][3], q)
        where = (pl.ds(q * lanes, lanes), pl.ds(lo, size))
        return pltpu.make_async_remote_copy(
            src_ref=source.at[where],
            dst_ref=targets[goal][0].at[where],
            send_sem=send_sem.at[len(order), q],
            recv_sem=recv_sem.at[order.index(goal), q],
            device_id=at(shift),
            device_id_type=MESH,
        )

    total = jnp.zeros((block // 2, lanes), F32)
    for q in range(strips):
        for r in (2 * q, 2 * q + 1):
            for m in range(span // 2):
                cs = slice(m * lanes, (m + 1) * lanes)
                pair = []
                for k in (2 * m, 2 * m + 1):
                    offset = k - r
                    if offset < 0 or offset > half:
                        pair.append(None)
                        continue
                    slot = tab[r, offset]
                    tile = x_ref[jnp.clip(slot, 0, half), r].astype(F32)
                    tile = jnp.where(slot >= 0, tile, 0.0)
                    if offset == 0:
                        total = total + jnp.where(on_diagonal, 2.0 * tile, 0.0) - tile * tile
                    else:
                        total = total - 2.0 * (tile * tile)
                    pair.append(tile)
                if pair[0] is None and pair[1] is None:
                    own[r * block : (r + 1) * block, cs] = jnp.zeros((block, lanes), BF16)
                    continue
                pair = [jnp.zeros((block // 2, lanes), F32) if t is None else t for t in pair]
                place = (r % 2) * (span // 2) + m
                stage[place, pl.ds(0, block // 2, stride=2), :] = jnp.where(left, pair[0], pltpu.roll(pair[1], block, 1))
                stage[place, pl.ds(1, block // 2, stride=2), :] = jnp.where(left, pltpu.roll(pair[0], block, 1), pair[1])
                own[r * block : (r + 1) * block, cs] = stage[place].astype(BF16)
        if q == 0:
            pl.semaphore_wait(barrier, len(peers))
        strip_copy("f1", q).start()
        strip_copy("d1", q).start()

        @pl.when(even_device)
        def _():
            strip_copy("e2", q).start()

        @pl.when(jnp.logical_not(even_device))
        def _():
            strip_copy("d2", q).start()

        strip_copy("e1", q).start()
        strip_copy("c1", q).start()

    part = total[0:8]
    for i in range(1, block // 16):
        part = part + total[8 * i : 8 * i + 8]

    def col_copy(d, mine):
        return pltpu.make_async_remote_copy(
            src_ref=col_parts.at[my_col],
            dst_ref=col_parts.at[my_col if mine else col_peer(ncol - d)],
            send_sem=col_send.at[d],
            recv_sem=col_recv.at[d],
            device_id=(my_row, col_peer(d)),
            device_id_type=MESH,
        )

    def row_copy(d, mine):
        return pltpu.make_async_remote_copy(
            src_ref=row_parts.at[my_row],
            dst_ref=row_parts.at[my_row if mine else row_peer(nrow - d)],
            send_sem=row_send.at[d],
            recv_sem=row_recv.at[d],
            device_id=(row_peer(d), my_col),
            device_id_type=MESH,
        )

    col_parts[my_col] = part
    for d in range(1, ncol):
        col_copy(d, True).start()

    def panel(i):
        return prod.at[:, i * width : (i + 1) * width]

    p0, p1, p2 = panel(0), panel(1), panel(2)
    d = own.at[:, :width]
    a = own.at[:, width : 2 * width]
    b = own.at[:, 2 * width :]

    corner = (
        lax.broadcasted_iota(jnp.int32, (lanes, lanes), 0) // block
        <= lax.broadcasted_iota(jnp.int32, (lanes, lanes), 1) // block
    )

    def symmetric_tile(upper):
        upper = upper.astype(F32)
        return jnp.where(corner, upper, upper.T).astype(BF16)

    def times_symmetric(x, u, p, q):
        lo, hi = q * lanes, (q + 1) * lanes
        rs = slice(lo, hi)
        tile = symmetric_tile(u[rs, lo:hi])
        p[:, rs] += dot(x[:, rs], tile, 1, 0)
        if hi < width:
            p[:, rs] += dot(x[:, hi:], u[rs, hi:], 1, 1)
            p[:, hi:] += dot(x[:, rs], u[rs, hi:], 1, 0)

    p0[...] = dot(a[...], a[...], 1, 1) + dot(b[...], b[...], 1, 1)
    full = d[...].astype(F32)
    block_upper = (
        lax.broadcasted_iota(jnp.int32, (width, width), 0) // block
        <= lax.broadcasted_iota(jnp.int32, (width, width), 1) // block
    )
    full = jnp.where(block_upper, full, full.T).astype(BF16)
    p0[...] += dot(full, full, 1, 0)
    p1[...] = dot(full, a[...], 1, 0)
    p2[...] = dot(full, b[...], 1, 0)

    for i in range(1, ncol):
        col_copy(i, False).wait_recv()
    part = col_parts[0]
    for i in range(1, ncol):
        part = part + col_parts[i]
    row_parts[my_row] = part
    for i in range(1, nrow):
        row_copy(i, True).start()

    for q in range(strips):
        rs = slice(q * lanes, (q + 1) * lanes)
        low = slice(0, (q + 1) * lanes)
        strip_copy("f1", q).wait_recv()

        @pl.when(even_device)
        def _():
            forward_copy("f1", q).start()

        strip_copy("d1", q).wait_recv()

        @pl.when(jnp.logical_not(even_device))
        def _():
            forward_copy("d1", q).start()

        times_symmetric(a, d1, p1, q)
        strip_copy("e1", q).wait_recv()
        p0[...] += dot(e1[rs, :], e1[rs, :], 0, 0)
        p1[:, low] += dot(e1[rs, :], f1[rs, low], 0, 0)
        strip_copy("c1", q).wait_recv()
        p1[:, rs] += dot(b[...], c1[rs, :], 1, 1)
        p2[...] += dot(a[:, rs], c1[rs, :], 1, 0)
    for q in range(strips):
        rs = slice(q * lanes, (q + 1) * lanes)
        low = slice(0, (q + 1) * lanes)
        strip_copy("e2", q).wait_recv()
        p0[low, low] += dot(e2[rs, low], e2[rs, low], 0, 0)
        strip_copy("d2", q).wait_recv()
        times_symmetric(b, d2, p2, q)

    for r in range(rows):
        for m in range(r // 2, (r + half) // 2 + 1):
            cs = slice(m * lanes, (m + 1) * lanes)
            place = (r % 2) * (span // 2) + m
            stage[place] = prod[r * block : (r + 1) * block, cs]
            even = stage[place, pl.ds(0, block // 2, stride=2), :]
            odd = stage[place, pl.ds(1, block // 2, stride=2), :]
            flat[r, 2 * m] = jnp.where(left, even, pltpu.roll(odd, block, 1))
            flat[r, 2 * m + 1] = jnp.where(left, pltpu.roll(even, block, 1), odd)

    def pick(r, carry):
        row_id = me * rows + r
        for s in range(slots):
            column = cols_ref[r, s]
            offset = column - row_id
            offset = jnp.where(offset < 0, offset + nblocks, offset)
            offset = jnp.where(column >= 0, jnp.minimum(offset, half), 0)
            fresh = 2.0 * x_ref[s, r].astype(F32) - flat[r, r + offset]
            out_ref[s, r] = jnp.where(column >= 0, fresh, 0.0)
        return carry

    lax.fori_loop(0, rows, pick, 0)

    for i in range(1, nrow):
        row_copy(i, False).wait_recv()
    part = row_parts[0]
    for i in range(1, nrow):
        part = part + row_parts[i]
    occupancy_ref[0, 0] = jnp.sum(part) * (1.0 / (nblocks * block))

    for q in range(strips):
        for name in ("f1", "d1", "e1", "c1"):
            strip_copy(name, q).wait_send()

        @pl.when(even_device)
        def _():
            strip_copy("e2", q).wait_send()
            forward_copy("f1", q).wait_send()

        @pl.when(jnp.logical_not(even_device))
        def _():
            strip_copy("d2", q).wait_send()
            forward_copy("d1", q).wait_send()

    for i in range(1, ncol):
        col_copy(i, True).wait_send()
    for i in range(1, nrow):
        row_copy(i, True).wait_send()


def body(nrow, ncol, upper_tiles, block_columns):
    rows, slots, tile_size = upper_tiles.shape
    block = math.isqrt(tile_size)
    half = slots - 1
    assert half == 2 * rows and rows % 2 == 0 and 2 * block == 128 and ncol % 2 == 0
    lanes = 2 * block
    width = rows * block
    span = rows + half
    strips = rows // 2

    square = pltpu.VMEM((width, width), BF16)
    new, occupancy = pl.pallas_call(
        functools.partial(kernel, (rows, slots, block, nrow, ncol)),
        out_shape=(
            jax.ShapeDtypeStruct((slots, rows, block // 2, lanes), F32),
            jax.ShapeDtypeStruct((1, 1), F32),
        ),
        in_specs=[pl.BlockSpec(memory_space=pltpu.VMEM), pl.BlockSpec(memory_space=pltpu.SMEM)],
        out_specs=(pl.BlockSpec(memory_space=pltpu.VMEM), pl.BlockSpec(memory_space=pltpu.SMEM)),
        scratch_shapes=[
            pltpu.SMEM((rows, slots), jnp.int32),
            pltpu.VMEM((span, block, lanes), F32),
            pltpu.VMEM((rows, span, block // 2, lanes), F32),
            pltpu.VMEM((width, 3 * width), BF16),
            square,
            square,
            square,
            square,
            square,
            square,
            pltpu.VMEM((width, 3 * width), F32),
            pltpu.VMEM((ncol, 8, lanes), F32),
            pltpu.VMEM((nrow, 8, lanes), F32),
            pltpu.SemaphoreType.DMA((7, strips)),
            pltpu.SemaphoreType.DMA((6, strips)),
            pltpu.SemaphoreType.DMA((ncol,)),
            pltpu.SemaphoreType.DMA((ncol,)),
            pltpu.SemaphoreType.DMA((nrow,)),
            pltpu.SemaphoreType.DMA((nrow,)),
        ],
        compiler_params=pltpu.CompilerParams(
            collective_id=0, has_side_effects=True, vmem_limit_bytes=48 * 1024 * 1024
        ),
        cost_estimate=pl.CostEstimate(
            flops=24 * width**3, bytes_accessed=6 * rows * slots * tile_size, transcendentals=0
        ),
    )(upper_tiles.swapaxes(0, 1).reshape(slots, rows, block // 2, lanes), block_columns)
    return new.reshape(slots, rows, tile_size).swapaxes(0, 1), occupancy[0, 0]


def solution(mesh):
    placed = (P(("row", "col"), None, None), P(("row", "col"), None))
    return jax.shard_map(
        functools.partial(body, mesh.shape["row"], mesh.shape["col"]),
        mesh=mesh,
        in_specs=placed,
        out_specs=(P(("row", "col"), None, None), P()),
        check_vma=False,
    )
```

time: 91.4 us -> 50.4 us (0.55); the launches traced: 89.8 us -> 49.9 us
  blocking collectives: 39.5 us -> 0 us
  Pallas kernels: 41 us -> 44.2 us
  other arithmetic: 2.18 us -> 0 us
  between operations: 3.78 us -> 2.43 us
    psum x1 -> x0, blocking collectives: 39.5 us -> none  [body(): total = lax.psum(doubled - squares, ('row', 'col'))]
    pallas_call x1, Pallas kernels: 41 us -> 44.2 us  [body(): pl.pallas_call(functools.partial(kernel, (rows, slots, block, nrow, ncol)...]
    reduce_sum x2 -> x0, other arithmetic: 1.94 us -> none  [the longest x1 1.3 us: body(): squares = jnp.sum(tiles * tiles * weight[:, :, None])]
where the time goes in v2:
time: 50.4 us; the launch traced here: 49.9 us
  Pallas kernels  44.2 us (88%)
  local copies, waits for them, and re-layouts  3.25 us (6%)
  between operations  2.43 us (5%)
    pallas_call x1, Pallas kernels, body(): pl.pallas_call(functools.partial(kernel, (rows, slots, block, nrow, ncol)...  44.2 us
    reshape x1, local copies, waits for them, and re-layouts, body(): return (new.reshape(slots, rows, tile_size).swapaxes(0, 1), occupancy[0, 0])  1.76 us
    unnamed x3, local copies, waits for them, and re-layouts  1.49 us

profile of v2, /device:TPU:1, one launch (start us, length us, event | category | flops | bytes accessed | tf_op | source)
XLA Modules:
  0.0 49.9 jit_solution(11706616380629025068)
XLA Ops:
  0.6 0.0 copy-start
  0.6 1.5 %copy.6 = bf16[17,8,32,128]{3,2,1,0:T(8,128)(2,1)S(1)} copy(bf16[17,8,32,128]{3,1,2,0:T(8,128)(2,1)} %bitcast.12) | data formatting | bytes 2228224
  2.1 0.0 copy-done
  2.1 44.2 %shard_map.41 = (f32[17,8,32,128]{3,2,1,0:T(8,128)S(1)}, f32[1,1]{1,0:T(1,128)}) custom-call(bf16[17,8,32,128]{3,2,1,0:T(8,128)(2,1)S(1)} %copy.6, s32[8,17]{1,0:T(8,128)S(1)} %copy-done), custom_call_target="tpu_custom_call" | custom-call | flops 3221225472 | bytes 3342336 | tf_op jit(solution)/shard_map/pallas_call | solution.py:336
  46.4 1.8 %reshape.11 = f32[17,8,4096]{2,1,0:T(8,128)} reshape(f32[17,8,32,128]{3,2,1,0:T(8,128)S(1)} %get-tuple-element.4) | data formatting | bytes 4456448 | tf_op jit(solution)/shard_map/reshape | solution.py:372
Async XLA Ops:
  0.6 1.5 %copy-start = (s32[8,17]{1,0:T(8,128)S(1)}, s32[8,17]{1,0:T(8,128)}, u32[]{:S(2)}) copy-start(s32[8,17]{1,0:T(8,128)} %cols_ref.1) | copy-start | bytes 1636

commit v3 on v2

--- a/solution.py
+++ b/solution.py
@@ -165,6 +165,7 @@
         def _():
             strip_copy("d2", q).start()
 
+    for q in range(strips):
         strip_copy("e1", q).start()
         strip_copy("c1", q).start()
 
@@ -233,6 +234,31 @@
     p1[...] = dot(full, a[...], 1, 0)
     p2[...] = dot(full, b[...], 1, 0)
 
+    def far(q):
+        low = slice(0, (q + 1) * lanes)
+        strip_copy("e2", q).wait_recv()
+        p0[low, low] += dot(e2[q * lanes : (q + 1) * lanes, low], e2[q * lanes : (q + 1) * lanes, low], 0, 0)
+        strip_copy("d2", q).wait_recv()
+        times_symmetric(b, d2, p2, q)
+
+    for q in range(strips):
+        strip_copy("f1", q).wait_recv()
+
+        @pl.when(even_device)
+        def _():
+            forward_copy("f1", q).start()
+
+        strip_copy("d1", q).wait_recv()
+
+        @pl.when(jnp.logical_not(even_device))
+        def _():
+            forward_copy("d1", q).start()
+
+        times_symmetric(a, d1, p1, q)
+        if q:
+            far(q - 1)
+    far(strips - 1)
+
     for i in range(1, ncol):
         col_copy(i, False).wait_recv()
     part = col_parts[0]
@@ -245,32 +271,12 @@
     for q in range(strips):
         rs = slice(q * lanes, (q + 1) * lanes)
         low = slice(0, (q + 1) * lanes)
-        strip_copy("f1", q).wait_recv()
-
-        @pl.when(even_device)
-        def _():
-            forward_copy("f1", q).start()
-
-        strip_copy("d1", q).wait_recv()
-
-        @pl.when(jnp.logical_not(even_device))
-        def _():
-            forward_copy("d1", q).start()
-
-        times_symmetric(a, d1, p1, q)
+        strip_copy("c1", q).wait_recv()
+        p1[:, rs] += dot(b[...], c1[rs, :], 1, 1)
+        p2[...] += dot(a[:, rs], c1[rs, :], 1, 0)
         strip_copy("e1", q).wait_recv()
         p0[...] += dot(e1[rs, :], e1[rs, :], 0, 0)
         p1[:, low] += dot(e1[rs, :], f1[rs, low], 0, 0)
-        strip_copy("c1", q).wait_recv()
-        p1[:, rs] += dot(b[...], c1[rs, :], 1, 1)
-        p2[...] += dot(a[:, rs], c1[rs, :], 1, 0)
-    for q in range(strips):
-        rs = slice(q * lanes, (q + 1) * lanes)
-        low = slice(0, (q + 1) * lanes)
-        strip_copy("e2", q).wait_recv()
-        p0[low, low] += dot(e2[rs, low], e2[rs, low], 0, 0)
-        strip_copy("d2", q).wait_recv()
-        times_symmetric(b, d2, p2, q)
 
     for r in range(rows):
         for m in range(r // 2, (r + half) // 2 + 1):

time: 50.4 us -> 46 us (0.913)
  Pallas kernels: 44.2 us -> 39.8 us
    pallas_call x1, Pallas kernels: 44.2 us -> 39.8 us  [body(): pl.pallas_call(functools.partial(kernel, (rows, slots, block, nrow, ncol)...]
where the time goes in v3:
time: 46 us; the launch traced here: 45.4 us
  Pallas kernels  39.8 us (87%)
  local copies, waits for them, and re-layouts  3.25 us (7%)
  between operations  2.43 us (5%)
    pallas_call x1, Pallas kernels, body(): pl.pallas_call(functools.partial(kernel, (rows, slots, block, nrow, ncol)...  39.8 us
    reshape x1, local copies, waits for them, and re-layouts, body(): return (new.reshape(slots, rows, tile_size).swapaxes(0, 1), occupancy[0, 0])  1.76 us
    unnamed x3, local copies, waits for them, and re-layouts  1.49 us

profile of v3, /device:TPU:1, one launch (start us, length us, event | category | flops | bytes accessed | tf_op | source)
XLA Modules:
  0.0 45.4 jit_solution(14333683021938661740)
XLA Ops:
  0.6 0.0 copy-start
  0.6 1.5 %copy.6 = bf16[17,8,32,128]{3,2,1,0:T(8,128)(2,1)S(1)} copy(bf16[17,8,32,128]{3,1,2,0:T(8,128)(2,1)} %bitcast.12) | data formatting | bytes 2228224
  2.1 0.0 copy-done
  2.1 39.8 %shard_map.41 = (f32[17,8,32,128]{3,2,1,0:T(8,128)S(1)}, f32[1,1]{1,0:T(1,128)}) custom-call(bf16[17,8,32,128]{3,2,1,0:T(8,128)(2,1)S(1)} %copy.6, s32[8,17]{1,0:T(8,128)S(1)} %copy-done), custom_call_target="tpu_custom_call" | custom-call | flops 3221225472 | bytes 3342336 | tf_op jit(solution)/shard_map/pallas_call | solution.py:342
  41.9 1.8 %reshape.11 = f32[17,8,4096]{2,1,0:T(8,128)} reshape(f32[17,8,32,128]{3,2,1,0:T(8,128)S(1)} %get-tuple-element.4) | data formatting | bytes 4456448 | tf_op jit(solution)/shard_map/reshape | solution.py:378
Async XLA Ops:
  0.6 1.5 %copy-start = (s32[8,17]{1,0:T(8,128)S(1)}, s32[8,17]{1,0:T(8,128)}, u32[]{:S(2)}) copy-start(s32[8,17]{1,0:T(8,128)} %cols_ref.1) | copy-start | bytes 1636

commit v4 on v3

--- a/solution.py
+++ b/solution.py
@@ -23,7 +23,6 @@
     cols_ref,
     out_ref,
     occupancy_ref,
-    tab,
     stage,
     flat,
     own,
@@ -73,19 +72,17 @@
     for peer in peers:
         pl.semaphore_signal(barrier, inc=1, device_id=peer, device_id_type=MESH)
 
-    def fill(r, carry):
+    def slots_of(r):
         row_id = me * rows + r
-        tab[r, 0] = jnp.where(cols_ref[r, 0] >= 0, 0, -1).astype(jnp.int32)
+        found = [jnp.where(cols_ref[r, 0] >= 0, 0, -1).astype(jnp.int32)]
         slot = jnp.int32(1)
         for offset in range(1, half + 1):
             want = row_id + offset
             want = jnp.where(want >= nblocks, want - nblocks, want)
             hit = cols_ref[r, jnp.minimum(slot, half)] == want
-            tab[r, offset] = jnp.where(hit, slot, -1)
+            found.append(jnp.where(hit, slot, -1))
             slot = slot + hit.astype(jnp.int32)
-        return carry
-
-    lax.fori_loop(0, rows, fill, 0)
+        return found
 
     sub = lax.broadcasted_iota(jnp.int32, (block // 2, lanes), 0)
     lane = lax.broadcasted_iota(jnp.int32, (block // 2, lanes), 1)
@@ -128,6 +125,7 @@
     total = jnp.zeros((block // 2, lanes), F32)
     for q in range(strips):
         for r in (2 * q, 2 * q + 1):
+            found = slots_of(r)
             for m in range(span // 2):
                 cs = slice(m * lanes, (m + 1) * lanes)
                 pair = []
@@ -136,7 +134,7 @@
                     if offset < 0 or offset > half:
                         pair.append(None)
                         continue
-                    slot = tab[r, offset]
+                    slot = found[offset]
                     tile = x_ref[jnp.clip(slot, 0, half), r].astype(F32)
                     tile = jnp.where(slot >= 0, tile, 0.0)
                     if offset == 0:
@@ -268,25 +266,47 @@
     for i in range(1, nrow):
         row_copy(i, True).start()
 
-    for q in range(strips):
+    def above(q):
         rs = slice(q * lanes, (q + 1) * lanes)
-        low = slice(0, (q + 1) * lanes)
         strip_copy("c1", q).wait_recv()
         p1[:, rs] += dot(b[...], c1[rs, :], 1, 1)
         p2[...] += dot(a[:, rs], c1[rs, :], 1, 0)
+
+    def below(q):
+        rs = slice(q * lanes, (q + 1) * lanes)
+        low = slice(0, (q + 1) * lanes)
         strip_copy("e1", q).wait_recv()
         p0[...] += dot(e1[rs, :], e1[rs, :], 0, 0)
         p1[:, low] += dot(e1[rs, :], f1[rs, low], 0, 0)
 
-    for r in range(rows):
-        for m in range(r // 2, (r + half) // 2 + 1):
-            cs = slice(m * lanes, (m + 1) * lanes)
-            place = (r % 2) * (span // 2) + m
-            stage[place] = prod[r * block : (r + 1) * block, cs]
-            even = stage[place, pl.ds(0, block // 2, stride=2), :]
-            odd = stage[place, pl.ds(1, block // 2, stride=2), :]
-            flat[r, 2 * m] = jnp.where(left, even, pltpu.roll(odd, block, 1))
-            flat[r, 2 * m + 1] = jnp.where(left, pltpu.roll(even, block, 1), odd)
+    def pack(first, last):
+        for r in range(rows):
+            for m in range(max(r // 2, first * strips), min((r + half) // 2, (last + 1) * strips - 1) + 1):
+                cs = slice(m * lanes, (m + 1) * lanes)
+                place = (r % 2) * (span // 2) + m
+                stage[place] = prod[r * block : (r + 1) * block, cs]
+                even = stage[place, pl.ds(0, block // 2, stride=2), :]
+                odd = stage[place, pl.ds(1, block // 2, stride=2), :]
+                flat[r, 2 * m] = jnp.where(left, even, pltpu.roll(odd, block, 1))
+                flat[r, 2 * m + 1] = jnp.where(left, pltpu.roll(even, block, 1), odd)
+
+    @pl.when(even_device)
+    def _():
+        for q in range(strips):
+            above(q)
+        pack(2, 2)
+        for q in range(strips):
+            below(q)
+        pack(0, 1)
+
+    @pl.when(jnp.logical_not(even_device))
+    def _():
+        for q in range(strips):
+            below(q)
+        pack(0, 0)
+        for q in range(strips):
+            above(q)
+        pack(1, 2)
 
     def pick(r, carry):
         row_id = me * rows + r
@@ -348,7 +368,6 @@
         in_specs=[pl.BlockSpec(memory_space=pltpu.VMEM), pl.BlockSpec(memory_space=pltpu.SMEM)],
         out_specs=(pl.BlockSpec(memory_space=pltpu.VMEM), pl.BlockSpec(memory_space=pltpu.SMEM)),
         scratch_shapes=[
-            pltpu.SMEM((rows, slots), jnp.int32),
             pltpu.VMEM((span, block, lanes), F32),
             pltpu.VMEM((rows, span, block // 2, lanes), F32),
             pltpu.VMEM((width, 3 * width), BF16),

time: 46 us -> 45.6 us (level)
  Pallas kernels: 39.8 us -> 39.3 us
where the time goes in v4:
time: 45.6 us; the launch traced here: 45 us
  Pallas kernels  39.3 us (86%)
  local copies, waits for them, and re-layouts  3.25 us (7%)
  between operations  2.43 us (5%)
    pallas_call x1, Pallas kernels, body(): pl.pallas_call(functools.partial(kernel, (rows, slots, block, nrow, ncol)...  39.3 us
    reshape x1, local copies, waits for them, and re-layouts, body(): return (new.reshape(slots, rows, tile_size).swapaxes(0, 1), occupancy[0, 0])  1.76 us
    unnamed x3, local copies, waits for them, and re-layouts  1.49 us

profile of v4, /device:TPU:1, one launch (start us, length us, event | category | flops | bytes accessed | tf_op | source)
XLA Modules:
  0.0 45.0 jit_solution(9486875031890480148)
XLA Ops:
  0.6 0.0 copy-start
  0.6 1.5 %copy.6 = bf16[17,8,32,128]{3,2,1,0:T(8,128)(2,1)S(1)} copy(bf16[17,8,32,128]{3,1,2,0:T(8,128)(2,1)} %bitcast.12) | data formatting | bytes 2228224
  2.1 0.0 copy-done
  2.1 39.3 %shard_map.41 = (f32[17,8,32,128]{3,2,1,0:T(8,128)S(1)}, f32[1,1]{1,0:T(1,128)}) custom-call(bf16[17,8,32,128]{3,2,1,0:T(8,128)(2,1)S(1)} %copy.6, s32[8,17]{1,0:T(8,128)S(1)} %copy-done), custom_call_target="tpu_custom_call" | custom-call | flops 3221225472 | bytes 3342336 | tf_op jit(solution)/shard_map/pallas_call | solution.py:362
  41.5 1.8 %reshape.11 = f32[17,8,4096]{2,1,0:T(8,128)} reshape(f32[17,8,32,128]{3,2,1,0:T(8,128)S(1)} %get-tuple-element.4) | data formatting | bytes 4456448 | tf_op jit(solution)/shard_map/reshape | solution.py:397
Async XLA Ops:
  0.6 1.5 %copy-start = (s32[8,17]{1,0:T(8,128)S(1)}, s32[8,17]{1,0:T(8,128)}, u32[]{:S(2)}) copy-start(s32[8,17]{1,0:T(8,128)} %cols_ref.1) | copy-start | bytes 1636

commit v5 on v4

--- a/solution.py
+++ b/solution.py
@@ -163,10 +163,6 @@
         def _():
             strip_copy("d2", q).start()
 
-    for q in range(strips):
-        strip_copy("e1", q).start()
-        strip_copy("c1", q).start()
-
     part = total[0:8]
     for i in range(1, block // 16):
         part = part + total[8 * i : 8 * i + 8]
@@ -232,31 +228,6 @@
     p1[...] = dot(full, a[...], 1, 0)
     p2[...] = dot(full, b[...], 1, 0)
 
-    def far(q):
-        low = slice(0, (q + 1) * lanes)
-        strip_copy("e2", q).wait_recv()
-        p0[low, low] += dot(e2[q * lanes : (q + 1) * lanes, low], e2[q * lanes : (q + 1) * lanes, low], 0, 0)
-        strip_copy("d2", q).wait_recv()
-        times_symmetric(b, d2, p2, q)
-
-    for q in range(strips):
-        strip_copy("f1", q).wait_recv()
-
-        @pl.when(even_device)
-        def _():
-            forward_copy("f1", q).start()
-
-        strip_copy("d1", q).wait_recv()
-
-        @pl.when(jnp.logical_not(even_device))
-        def _():
-            forward_copy("d1", q).start()
-
-        times_symmetric(a, d1, p1, q)
-        if q:
-            far(q - 1)
-    far(strips - 1)
-
     for i in range(1, ncol):
         col_copy(i, False).wait_recv()
     part = col_parts[0]
@@ -265,6 +236,35 @@
     row_parts[my_row] = part
     for i in range(1, nrow):
         row_copy(i, True).start()
+
+    for q in range(strips):
+        strip_copy("e1", q).start()
+        strip_copy("c1", q).start()
+
+    def far(q):
+        low = slice(0, (q + 1) * lanes)
+        strip_copy("e2", q).wait_recv()
+        p0[low, low] += dot(e2[q * lanes : (q + 1) * lanes, low], e2[q * lanes : (q + 1) * lanes, low], 0, 0)
+        strip_copy("d2", q).wait_recv()
+        times_symmetric(b, d2, p2, q)
+
+    for q in range(strips):
+        strip_copy("f1", q).wait_recv()
+
+        @pl.when(even_device)
+        def _():
+            forward_copy("f1", q).start()
+
+        strip_copy("d1", q).wait_recv()
+
+        @pl.when(jnp.logical_not(even_device))
+        def _():
+            forward_copy("d1", q).start()
+
+        times_symmetric(a, d1, p1, q)
+        if q:
+            far(q - 1)
+    far(strips - 1)
 
     def above(q):
         rs = slice(q * lanes, (q + 1) * lanes)

time: 45.6 us -> 43.3 us (0.950)
  Pallas kernels: 39.3 us -> 37.5 us
    pallas_call x1, Pallas kernels: 39.3 us -> 37.5 us  [body(): pl.pallas_call(functools.partial(kernel, (rows, slots, block, nrow, ncol)...]
where the time goes in v5:
time: 43.3 us; the launch traced here: 43.1 us
  Pallas kernels  37.5 us (87%)
  local copies, waits for them, and re-layouts  3.25 us (8%)
  between operations  2.43 us (6%)
    pallas_call x1, Pallas kernels, body(): pl.pallas_call(functools.partial(kernel, (rows, slots, block, nrow, ncol)...  37.5 us
    reshape x1, local copies, waits for them, and re-layouts, body(): return (new.reshape(slots, rows, tile_size).swapaxes(0, 1), occupancy[0, 0])  1.76 us
    unnamed x3, local copies, waits for them, and re-layouts  1.49 us

profile of v5, /device:TPU:1, one launch (start us, length us, event | category | flops | bytes accessed | tf_op | source)
XLA Modules:
  0.0 43.1 jit_solution(11019520275688491470)
XLA Ops:
  0.6 0.0 copy-start
  0.6 1.5 %copy.6 = bf16[17,8,32,128]{3,2,1,0:T(8,128)(2,1)S(1)} copy(bf16[17,8,32,128]{3,1,2,0:T(8,128)(2,1)} %bitcast.12) | data formatting | bytes 2228224
  2.1 0.0 copy-done
  2.1 37.5 %shard_map.41 = (f32[17,8,32,128]{3,2,1,0:T(8,128)S(1)}, f32[1,1]{1,0:T(1,128)}) custom-call(bf16[17,8,32,128]{3,2,1,0:T(8,128)(2,1)S(1)} %copy.6, s32[8,17]{1,0:T(8,128)S(1)} %copy-done), custom_call_target="tpu_custom_call" | custom-call | flops 3221225472 | bytes 3342336 | tf_op jit(solution)/shard_map/pallas_call | solution.py:362
  39.6 1.8 %reshape.11 = f32[17,8,4096]{2,1,0:T(8,128)} reshape(f32[17,8,32,128]{3,2,1,0:T(8,128)S(1)} %get-tuple-element.4) | data formatting | bytes 4456448 | tf_op jit(solution)/shard_map/reshape | solution.py:397
Async XLA Ops:
  0.6 1.5 %copy-start = (s32[8,17]{1,0:T(8,128)S(1)}, s32[8,17]{1,0:T(8,128)}, u32[]{:S(2)}) copy-start(s32[8,17]{1,0:T(8,128)} %cols_ref.1) | copy-start | bytes 1636
